TPU v7x, 256 devices: a whole 4x4x8 slice. The times are simulated.
256 devices in a mesh: cube: 8 (over y, x_lo), grid: 32 (over x_hi, z, core).
Axes of the slice: x: 4 (x_hi: 2, x_lo: 2; x = x_hi * 2 + x_lo), y: 4, z: 8, core: 2. Of those that a mesh axis runs over, the one named last changes fastest.
Arguments:
- panel: float32 [8, 2048, 512], P('cube', 'grid'), may hold values from -0.25 to 0.25
- pattern: int32 [8, 8, 2], P('cube'), may hold values 0 or 1
- child_inverse: float32 [8, 512, 512], P('cube'), as said below
- ext_map: int32 [8, 8], replicated, may hold values from 0 to 17, as said below
- upper_rows: float32 [8, 2048, 512], P('cube', 'grid'), may hold values from -0.625 to 0.625
- parent_inverse: float32 [8, 256, 512], P('cube'), as said below
- update_block: float32 [8, 2048, 4096], P('cube', None, 'grid'), as said below
Outputs:
- schur: float32 [8, 2048, 4096], P('cube', None, 'grid')
Inputs may be any that keep to these rules, and one draw needn't show every extreme that they name: `ext_map`: within each row the 8 entries are distinct parent tiles. Each child_inverse[c] is lower triangular with positive diagonal. `parent_inverse`: each parent's two halves together form a lower triangular matrix with positive diagonal. `update_block`: each parent's two halves together form a symmetric matrix.
All inputs are finite; a program needn't handle non-finite values. No bound on the sum of `pattern` on one device may be relied on, other than what follows from the above.
Results may differ from a plain program's by a relative error of at most 0.00011.
Values sent between devices are 32-bit elements; how exact they have to be, the bound alone decides.
A program may use at most 128 MiB of HBM per device.

v0:
```python
import jax
import jax.numpy as jnp
from jax import lax
from jax.sharding import PartitionSpec as P

TILE = 256
PP = 512


def from_partner(value, axis, bit):
    mask = 2**bit
    pairs = [(source, source ^ mask) for source in range(lax.axis_size(axis))]
    return lax.ppermute(value, axis, pairs)


def product(left, right):
    return jnp.dot(left, right, precision=lax.Precision.HIGHEST, preferred_element_type=jnp.float32)


def child_rows(panel_rows, pattern_rows, inverse, start_row, tile_size):
    row_count = panel_rows.shape[0]
    row_ids = start_row + jnp.arange(row_count, dtype=jnp.int32)
    own_tile = row_ids // tile_size
    select = (
        own_tile[:, None] == jnp.arange(pattern_rows.shape[0], dtype=jnp.int32)[None, :]
    ).astype(jnp.float32)
    keep_mask = product(select, pattern_rows.astype(jnp.float32))
    keep_mask = jnp.repeat(keep_mask, tile_size, axis=1)
    return product(panel_rows * keep_mask, inverse.T)


def extend_rows(panel_t, tile_map, row_ids, tile_size):
    parent_tile = row_ids // tile_size
    matches = parent_tile[:, None] == tile_map[None, :]
    present = jnp.sum(matches.astype(jnp.int32), axis=1)
    positions = jnp.arange(tile_map.shape[0], dtype=jnp.int32)[None, :]
    source_tile = jnp.sum(jnp.where(matches, positions, jnp.zeros_like(positions)), axis=1)
    source = source_tile * tile_size + row_ids % tile_size
    picked = jnp.take(panel_t, source, axis=0)
    return jnp.where(present[:, None] > 0, picked, jnp.zeros_like(picked))


def local(panel, pattern, child_inverse, ext_map, upper_rows, parent_inverse, update_block):
    grid_pos = lax.axis_index("grid")
    cube_pos = lax.axis_index("cube")
    half_pos = cube_pos % 2
    first_cube = cube_pos - half_pos
    local_count = panel.shape[1]
    own_wt = child_rows(panel[0], pattern[0], child_inverse[0], grid_pos * local_count, TILE)
    sibling_wt = from_partner(own_wt, "cube", 0)
    own_full, sibling_full = (
        lax.all_gather(own_wt, "grid", axis=0, tiled=True),
        lax.all_gather(sibling_wt, "grid", axis=0, tiled=True),
    )
    even_full = jnp.where(half_pos == 0, own_full, sibling_full)
    odd_full = jnp.where(half_pos == 0, sibling_full, own_full)
    even_map = lax.dynamic_index_in_dim(ext_map, first_cube, 0, keepdims=False)
    odd_map = lax.dynamic_index_in_dim(ext_map, first_cube + 1, 0, keepdims=False)

    def front_rows(row_ids):
        return jnp.concatenate(
            [
                extend_rows(even_full, even_map, row_ids, TILE),
                extend_rows(odd_full, odd_map, row_ids, TILE),
            ],
            axis=1,
        )

    half_rows = update_block.shape[1]
    column_count = update_block.shape[2]
    upper_count = upper_rows.shape[1]
    front_pivot = front_rows(jnp.arange(PP, dtype=jnp.int32))
    front_half = front_rows(PP + half_pos * half_rows + jnp.arange(half_rows, dtype=jnp.int32))
    front_cols = front_rows(
        PP + grid_pos * column_count + jnp.arange(column_count, dtype=jnp.int32)
    )
    front_local = lax.dynamic_slice_in_dim(front_half, grid_pos * upper_count, upper_count, 0)
    own_inverse = parent_inverse[0]
    other_inverse = from_partner(own_inverse, "cube", 0)
    pivot_inv = jnp.where(
        half_pos == 0,
        jnp.concatenate([own_inverse, other_inverse], axis=0),
        jnp.concatenate([other_inverse, own_inverse], axis=0),
    )
    upper_hat = upper_rows[0] - product(front_local, front_pivot.T)
    parent_wt = product(upper_hat, pivot_inv.T)
    column_start = grid_pos * column_count
    column_half = column_start // half_rows
    column_offset = column_start - column_half * half_rows
    other_wt = from_partner(parent_wt, "cube", 0)
    own_half, other_half = (
        lax.all_gather(parent_wt, "grid", axis=0, tiled=True),
        lax.all_gather(other_wt, "grid", axis=0, tiled=True),
    )
    column_source = jnp.where(column_half == half_pos, own_half, other_half)
    parent_cols = lax.dynamic_slice_in_dim(column_source, column_offset, column_count, 0)
    schur_local = (
        update_block[0] - product(front_half, front_cols.T) - product(own_half, parent_cols.T)
    )
    return schur_local[None]


def solution(mesh):
    in_specs = (
        P("cube", "grid", None),
        P("cube", None, None),
        P("cube", None, None),
        P(),
        P("cube", "grid", None),
        P("cube", None, None),
        P("cube", None, "grid"),
    )
    out_specs = P("cube", None, "grid")
    return jax.shard_map(local, mesh=mesh, in_specs=in_specs, out_specs=out_specs, check_vma=False)
```

profile of v0, /device:TPU:1, one launch (start us, length us, event | category | flops | bytes accessed | tf_op | source)
XLA Modules:
  0.0 426.0 jit_solution(2691086444114093837)
XLA Ops:
  6.6 1.0 fusion.32
  7.8 2.7 fusion.16
  10.5 2.1 collective-permute-start
  12.7 2.6 collective-permute-done
  15.9 1.5 collective-permute-start.1
  17.5 0.8 fusion.59
  18.7 83.2 %all-gather.5.cloned.1.call-done = f32[2048,512]{1,0:T(8,128)} async-done(((f32[64,512]{1,0:T(8,128)}), f32[2048,512]{1,0:T(8,128)}) %all-gather.5.cloned.1.call-update) | async-done | bytes 4194320 | tf_op jit(solution)/shard_map/all_gather | solution.py:52
  101.8 86.3 %all-gather.7.cloned.1.call-done = f32[2048,512]{1,0:T(8,128)} async-done(((f32[64,512]{1,0:T(8,128)}), f32[2048,512]{1,0:T(8,128)}) %all-gather.7.cloned.1.call-update) | async-done | bytes 4194320 | tf_op jit(solution)/shard_map/all_gather | solution.py:53
  188.1 8.1 %broadcast_select_fusion.1 = (f32[2048,512]{1,0:T(8,128)}, f32[2048,512]{1,0:T(8,128)}) fusion(f32[2048,512]{1,0:T(8,128)} %all-gather.5.cloned.1.call-done, f32[2048,512]{1,0:T(8,128)} %all-gather.7.cloned.1.call-done, pred[]{:T(512)S(6)} %eq.114), kind=kLoop, calls=%fused_computation.20 | loop fusion | flops 2097152 | bytes 16777216 | tf_op jit(solution)/shard_map/jit(_where)/select_n | solution.py:55
  196.2 4.2 gather_fusion.4
  200.5 11.7 %gather_fusion = f32[2048,512]{1,0:T(8,128)} fusion(f32[2048,512]{1,0:T(8,128)} %get-tuple-element.30, s32[2048]{0:T(1024)S(1)} %get-tuple-element.47), kind=kCustom, calls=%fused_computation.clone | custom fusion | bytes 8396800 | tf_op jit(solution)/shard_map/jit(_take)/gather | solution.py:39
  212.2 11.7 %gather_fusion.1 = f32[2048,512]{1,0:T(8,128)} fusion(f32[2048,512]{1,0:T(8,128)} %get-tuple-element.31, s32[2048]{0:T(1024)S(1)} %get-tuple-element.46), kind=kCustom, calls=%fused_computation.3.clone | custom fusion | bytes 8396800 | tf_op jit(solution)/shard_map/jit(_take)/gather | solution.py:39
  223.9 4.1 select_select_fusion.1
  228.4 3.5 select_select_fusion
  232.2 4.2 gather_fusion.5
  236.7 3.2 fusion.7
  239.9 3.0 fusion.10
  243.5 4.8 %collective-permute-done.2 = f32[64,512]{1,0:T(8,128)S(1)} collective-permute-done((f32[64,512]{1,0:T(8,128)}, f32[64,512]{1,0:T(8,128)S(1)}, u32[]{:S(2)}, u32[]{:S(2)}) %collective-permute-start.2) | collective-permute-done | bytes 131104 | tf_op jit(solution)/shard_map/ppermute | solution.py:13
  249.1 3.1 gather_fusion.2
  252.2 3.1 gather_fusion.3
  255.5 9.1 %fusion.2 = f32[2048,128]{1,0:T(8,128)S(1)} fusion(f32[2048,512]{1,0:T(8,128)} %select_select_fusion, f32[2048,512]{1,0:T(8,128)} %select_select_fusion.1, f32[1,2048,128]{2,1,0:T(8,128)S(1)} %copy-done.2, f32[128,512]{1,0:T(8,128)S(1)} %select_select_fusion.4, f32[128,512]{1,0:T(8,128)S(1)} %select_select_fusion.5), kind=kOutput, calls=%fused_computation.14 | convolution fusion | flops 3223715840 | bytes 11010048 | tf_op jit(solution)/shard_map/dot_general | solution.py:17
  264.6 61.9 %all-gather.9.cloned.1.call-done = f32[2048,512]{1,0:T(8,128)} async-done(((f32[64,512]{1,0:T(8,128)}), f32[2048,512]{1,0:T(8,128)}) %all-gather.9.cloned.1.call-update) | async-done | bytes 4194320 | tf_op jit(solution)/shard_map/all_gather | solution.py:92
  326.6 86.2 %all-gather.11.cloned.1.call-done = f32[2048,512]{1,0:T(8,128)} async-done(((f32[64,512]{1,0:T(8,128)}), f32[2048,512]{1,0:T(8,128)}) %all-gather.11.cloned.1.call-update) | async-done | bytes 4194320 | tf_op jit(solution)/shard_map/all_gather | solution.py:93
  412.7 6.7 %fusion.1 = f32[1,2048,128]{2,1,0:T(8,128)} fusion(f32[2048,128]{1,0:T(8,128)S(1)} %fusion.2, f32[2048,512]{1,0:T(8,128)} %all-gather.9.cloned.1.call-done, f32[2048,512]{1,0:T(8,128)} %all-gather.11.cloned.1.call-done, s32[]{:T(128)S(6)} %select_n.208, pred[]{:T(512)S(6)} %eq.131), kind=kOutput, calls=%fused_computation.13 | convolution fusion | flops 1610940416 | bytes 6815749 | tf_op jit(solution)/shard_map/dot_general | solution.py:17
  (49 shorter events, 3.8 us)
Async XLA Ops:
  6.5 1.2 copy-start
  6.5 95.3 %all-gather.5.cloned.1.call-start = ((), (), s32[]{:S(2)}) async-start(), calls=%async_computation | async-start | bytes 4325376 | tf_op jit(solution)/shard_map/all_gather | solution.py:52
  10.5 177.7 %all-gather.7.cloned.1.call-start = ((), (), s32[]{:S(2)}) async-start(), calls=%async_computation.1 | async-start | bytes 4325376 | tf_op jit(solution)/shard_map/all_gather | solution.py:53
  10.5 4.7 %collective-permute-start = (f32[64,512]{1,0:T(8,128)}, f32[64,512]{1,0:T(8,128)S(1)}, u32[]{:S(2)}, u32[]{:S(2)}) collective-permute-start(f32[64,512]{1,0:T(8,128)} %fusion.16), channel_id=1, source_target_pairs={{0,32},{32,0},{64,96},{96,64},{128,160},{160,128},{192,224},{224,1... | collective-permute-start | bytes 393224 | tf_op jit(solution)/shard_map/ppermute | solution.py:13
  15.2 0.6 copy-start.4
  15.9 310.7 %all-gather.9.cloned.1.call-start = ((), (), s32[]{:S(2)}) async-start(), calls=%async_computation.2 | async-start | bytes 4325376 | tf_op jit(solution)/shard_map/all_gather | solution.py:92
  15.9 223.9 %collective-permute-start.1 = (f32[256,512]{1,0:T(8,128)}, f32[256,512]{1,0:T(8,128)}, u32[]{:S(2)}, u32[]{:S(2)}) collective-permute-start(f32[256,512]{1,0:T(8,128)} %bitcast.22), channel_id=1, source_target_pairs={{0,32},{32,0},{64,96},{96,64},{128,160},{160,128},{192,224},{224,1... | collective-permute-start | bytes 1572872 | tf_op jit(solution)/shard_map/ppermute | solution.py:13
  223.9 4.5 %copy-start.1 = (f32[2048,512]{1,0:T(8,128)S(1)}, f32[2048,512]{1,0:T(8,128)}, u32[]{:S(2)}) copy-start(f32[2048,512]{1,0:T(8,128)} %gather_fusion.1) | copy-start | bytes 12582916
  232.2 4.5 %copy-start.3 = (f32[1,64,512]{2,1,0:T(8,128)S(1)}, f32[1,64,512]{2,1,0:T(8,128)}, u32[]{:S(2)}) copy-start(f32[1,64,512]{2,1,0:T(8,128)} %param.17) | copy-start | bytes 393220
  236.6 3.2 copy-start.6
  239.8 15.7 %copy-start.2 = (f32[1,2048,128]{2,1,0:T(8,128)S(1)}, f32[1,2048,128]{2,1,0:T(8,128)}, u32[]{:S(2)}) copy-start(f32[1,2048,128]{2,1,0:T(8,128)} %param.19) | copy-start | bytes 3145732
  242.9 169.8 %all-gather.11.cloned.1.call-start = ((), (), s32[]{:S(2)}) async-start(), calls=%async_computation.3 | async-start | bytes 4325376 | tf_op jit(solution)/shard_map/all_gather | solution.py:93
  243.0 5.3 %collective-permute-start.2 = (f32[64,512]{1,0:T(8,128)}, f32[64,512]{1,0:T(8,128)S(1)}, u32[]{:S(2)}, u32[]{:S(2)}) collective-permute-start(f32[64,512]{1,0:T(8,128)} %fusion.10), channel_id=1, source_target_pairs={{0,32},{32,0},{64,96},{96,64},{128,160},{160,128},{192,224},{224,1... | collective-permute-start | bytes 393224 | tf_op jit(solution)/shard_map/ppermute | solution.py:13
  248.3 0.7 copy-start.5
Sparse Core Ops, SparseCore 0:
  10.6 91.1 all-gather.4
  104.6 83.4 all-gather.6
  243.0 83.4 all-gather.8
  329.2 83.4 all-gather.10
where the time goes:
time: 426 us
  waiting for transfers between devices  325 us (76%)
  local copies, waits for them, and re-layouts  40.8 us (10%)
  matrix products  25.6 us (6%)
  other arithmetic  16.8 us (4%)
  between operations  13.4 us (3%)
  starting transfers between devices  4.36 us (1%)
    all_gather x1, waiting for transfers between devices, local(): lax.all_gather(sibling_wt, 'grid', axis=0, tiled=True)  86.3 us
    all_gather x1, waiting for transfers between devices, local(): lax.all_gather(other_wt, 'grid', axis=0, tiled=True)  86.2 us
    all_gather x1, waiting for transfers between devices, local(): lax.all_gather(own_wt, 'grid', axis=0, tiled=True)  83.2 us
    all_gather x1, waiting for transfers between devices, local(): lax.all_gather(parent_wt, 'grid', axis=0, tiled=True)  61.9 us
    gather x6, local copies, waits for them, and re-layouts, extend_rows(): picked = jnp.take(panel_t, source, axis=0)  38.1 us
    dot_general x6, matrix products, product(): jnp.dot(left, right, precision=lax.Precision.HIGHEST, preferred_element_t...  25.6 us
  transfers between devices with their start and end apart: 7, of which 6 were waited for; matrix products, arithmetic and copies ran while one was open for 16% of the time, Pallas kernels for 0%

commit v1 on v0

v1 whole, which is shorter than its diff:
```python
import jax
import jax.numpy as jnp
from jax import lax
from jax.experimental import pallas as pl
from jax.experimental.pallas import tpu as pltpu
from jax.sharding import PartitionSpec as P

MESH = pl.DeviceIdType.MESH
F32 = jnp.float32
BF16 = jnp.bfloat16
NX, NZ = 4, 8
ROWS = 64
TILE = 256


def nt(left, right):
    return lax.dot_general(left, right, (((1,), (1,)), ((), ())), preferred_element_type=F32)


def nn(left, right):
    return lax.dot_general(left, right, (((1,), (0,)), ((), ())), preferred_element_type=F32)


def split(value):
    high = value.astype(BF16)
    return high, (value - high.astype(F32)).astype(BF16)


def stack(value):
    return jnp.concatenate(split(value), axis=0)


def dot3(mul, left, right_high, right_low):
    count = left.shape[0]
    both = stack(left)
    wide = mul(both, right_high)
    return wide[:count] + wide[count:] + mul(both[:count], right_low)


class Wires:
    def __init__(self, send_sems, recv_sems, any_device):
        self.send_sems, self.recv_sems, self.any_device = send_sems, recv_sems, any_device
        self.number, self.started = {}, []

    def copy(self, name, source, target, device):
        index = self.number.setdefault(name, len(self.number))
        return pltpu.make_async_remote_copy(
            src_ref=source,
            dst_ref=target,
            send_sem=self.send_sems.at[index],
            recv_sem=self.recv_sems.at[index],
            device_id=device,
            device_id_type=MESH,
        )

    def send(self, name, source, target, device):
        copy = self.copy(name, source, target, device)
        copy.start()
        self.started.append(copy)

    def arrive(self, name, target):
        self.copy(name, target, target, self.any_device).wait_recv()

    def drain(self):
        for copy in self.started:
            copy.wait_send()


def kernel(
    ext_ref, pat_ref, panel_ref, cinv_ref, upper_ref, pinv_ref, block_ref, out_ref,
    cbuf, ubuf, ucols, gbuf, panel_v, cinv_v, block_v, out_v,
    p_high, p_low, g_high, g_low, b_cat, y_cat, local_sems, out_sems, send_sems, recv_sems,
):
    cube, grid = lax.axis_index("cube"), lax.axis_index("grid")
    y, low = cube // 2, cube % 2
    high, z, core = grid // 16, (grid % 16) // 2, grid % 2
    x = high * 2 + low

    def device(xx, zz, cc):
        return (y * 2 + xx % 2, (xx // 2) * 16 + zz * 2 + cc)

    sibling = device(x, z, 1 - core)
    x_next = {1: device((x + 1) % NX, z, core), -1: device((x + 3) % NX, z, core)}
    x_far = device((x + 2) % NX, z, core)
    z_next = {1: device(x, (z + 1) % NZ, core), -1: device(x, (z + 7) % NZ, core)}

    def rows_of(xx, zz, cc, first, count):
        tile = (xx // 2) * 4 + zz // 2
        start = pl.multiple_of((zz % 2) * 128 + cc * ROWS + first, 8)
        return tile, pl.ds(start, count)

    def c_slot(dx, dz, cc, first=0, count=ROWS):
        xx, zz = (x + dx + NX) % NX, (z + dz + NZ) % NZ
        tile, rows = rows_of(xx, zz, cc, first, count)
        return cbuf.at[xx % 2, tile, rows]

    def u_slot(dx, dz, cc, first=0, count=ROWS):
        xx, zz = (x + dx + NX) % NX, (z + dz + NZ) % NZ
        tile, rows = rows_of(xx, zz, cc, first, count)
        return ubuf.at[tile, rows]

    loads = [
        pltpu.make_async_copy(panel_ref.at[0], panel_v, local_sems.at[0]),
        pltpu.make_async_copy(cinv_ref.at[0], cinv_v, local_sems.at[1]),
        pltpu.make_async_copy(upper_ref.at[0], u_slot(0, 0, core), local_sems.at[2]),
        pltpu.make_async_copy(
            pinv_ref.at[0], gbuf.at[pl.ds(pl.multiple_of(low * 256, 256), 256)], local_sems.at[3]
        ),
        pltpu.make_async_copy(block_ref.at[0], block_v, local_sems.at[4]),
    ]
    for load in loads:
        load.start()

    barrier = pltpu.get_barrier_semaphore()
    greeted = [sibling, x_next[1], x_next[-1], x_far, z_next[1], z_next[-1]]
    for other in greeted:
        pl.semaphore_signal(barrier, inc=1, device_id=other, device_id_type=MESH)
    pl.semaphore_wait(barrier, len(greeted))

    wires = Wires(send_sems, recv_sems, sibling)

    loads[2].wait()
    own_u = u_slot(0, 0, core)
    wires.send(("u", "far"), own_u, own_u, x_far)
    for way in (1, -1):
        wires.send(("u", 0, way, 1), own_u, own_u, z_next[way])
    wires.send(("u", "own", "pair"), own_u, own_u, sibling)

    loads[3].wait()

    def g_rows(half, way, cc):
        start = half * 256 + (0 if way == 1 else 128) + cc * 64
        return gbuf.at[pl.ds(pl.multiple_of(start, 64), 64)]

    for way in (1, -1):
        wires.send(("g", way), g_rows(low, way, core), g_rows(low, way, core), x_next[way])

    loads[0].wait()
    loads[1].wait()
    own_tile = grid // 4
    keep = [pat_ref[0, own_tile, part].astype(F32) for part in range(2)]
    masked = jnp.concatenate([panel_v[:, :256] * keep[0], panel_v[:, 256:] * keep[1]], axis=1)
    inv_high, inv_low = split(cinv_v[...])
    tile, rows = rows_of(x, z, core, 0, ROWS)
    cbuf[low, tile, rows, :] = dot3(nt, masked, inv_high, inv_low)

    half = ROWS // 2

    def span(step, way):
        if step < NZ // 2:
            return 0, ROWS
        return (0, half) if way == 1 else (half, half)

    def c_start_x(step, way):
        first, count = span(step, way)
        piece = c_slot(0, -way * step, core, first, count)
        for side in (1, -1):
            wires.send(("c", step, way, "x", side), piece, piece, x_next[side])

    def c_pair(name, piece):
        wires.send(name + ("pair",), piece, piece, sibling)

    def c_mid_x(step, way):
        first, count = span(step, way)
        for side in (1, -1):
            piece = c_slot(-side, -way * step, core, first, count)
            wires.arrive(("c", step, way, "x", side), piece)
            part = c_slot(-side, -way * step, core, first + (0 if side == 1 else count // 2), count // 2)
            wires.send(("c", step, way, "xx", side), part, part, x_next[side])
            c_pair(("c", step, way, "x", side), piece)

    def c_end_x(step, way):
        first, count = span(step, way)
        for side in (1, -1):
            part = c_slot(2, -way * step, core, first + (0 if side == 1 else count // 2), count // 2)
            wires.arrive(("c", step, way, "xx", side), part)
            c_pair(("c", step, way, "xx", side), part)

    def ring(kind, slot, step, way):
        first, count = span(step, way)
        piece = slot(-way * step, first, count)
        wires.arrive(kind + (way, step), piece)
        if step < NZ // 2:
            first, count = span(step + 1, way)
            part = slot(-way * step, first, count)
            wires.send(kind + (way, step + 1), part, part, z_next[way])
        wires.send(kind + (way, step, "pair"), piece, piece, sibling)

    def u_ring(dx, step, way):
        ring(("u", dx), lambda dz, first, count: u_slot(dx, dz, core, first, count), step, way)

    own_c = c_slot(0, 0, core)
    c_start_x(0, 1)
    for way in (1, -1):
        wires.send(("c", "z", way, 1), own_c, own_c, z_next[way])
    wires.send(("c", "own", "pair"), own_c, own_c, sibling)

    far_u = u_slot(2, 0, core)
    wires.arrive(("u", "far"), far_u)
    for way in (1, -1):
        wires.send(("u", 2, way, 1), far_u, far_u, z_next[way])
    wires.send(("u", "far", "pair"), far_u, far_u, sibling)
    for way in (1, -1):
        wires.arrive(("g", way), g_rows(1 - low, way, core))
        wires.send(("g", way, "pair"), g_rows(1 - low, way, core), g_rows(1 - low, way, core), sibling)

    rounds = [[(0, 1)]] + [[(step, 1), (step, -1)] for step in range(1, NZ // 2 + 1)]
    for step in range(1, len(rounds) + 2):
        if step < len(rounds):
            for _, way in rounds[step]:
                ring(("c", "z"), lambda dz, first, count: c_slot(0, dz, core, first, count), step, way)
                c_start_x(step, way)
            for _, way in rounds[step]:
                u_ring(0, step, way)
        if step - 1 < len(rounds):
            for pair in rounds[step - 1]:
                c_mid_x(*pair)
        if step < len(rounds):
            for _, way in rounds[step]:
                u_ring(2, step, way)
        if 0 <= step - 2 < len(rounds):
            for pair in rounds[step - 2]:
                c_end_x(*pair)

    other = 1 - core
    wires.arrive(("u", "own", "pair"), u_slot(0, 0, other))
    wires.arrive(("u", "far", "pair"), u_slot(2, 0, other))
    for dx in (0, 2):
        for step in range(1, NZ // 2 + 1):
            for way in (1, -1):
                wires.arrive(("u", dx, way, step, "pair"), u_slot(dx, -way * step, other, *span(step, way)))

    column_tile = high * 4 * 2 + z
    own_cols = low == high
    inner = jnp.logical_not(own_cols)
    tile_in_half = z
    col_rows = pl.multiple_of(core * 128, 128)

    @pl.when(own_cols)
    def _():
        ucols[...] = ubuf[tile_in_half, pl.ds(col_rows, 128), :]

    def cols_copy(way):
        first = 0 if way == 1 else ROWS
        return wires.copy(
            ("cols", way),
            ubuf.at[tile_in_half, pl.ds(pl.multiple_of(col_rows + first, 64), ROWS)],
            ucols.at[pl.ds(first, ROWS)],
            x_next[way],
        )

    def cols_needed(xx):
        return jnp.logical_or(xx == 1, xx == 2)

    for way in (1, -1):
        @pl.when(cols_needed((x + way + NX) % NX))
        def _(way=way):
            cols_copy(way).start()

    for way in (1, -1):
        wires.arrive(("g", way, "pair"), g_rows(1 - low, way, other))

    wires.arrive(("c", "own", "pair"), c_slot(0, 0, other))
    for step in range(1, NZ // 2 + 1):
        for way in (1, -1):
            wires.arrive(("c", "z", way, step, "pair"), c_slot(0, -way * step, other, *span(step, way)))
    for pairs in rounds:
        for step, way in pairs:
            first, count = span(step, way)
            for side in (1, -1):
                wires.arrive(
                    ("c", step, way, "x", side, "pair"), c_slot(-side, -way * step, other, first, count)
                )
                part = c_slot(2, -way * step, other, first + (0 if side == 1 else count // 2), count // 2)
                wires.arrive(("c", step, way, "xx", side, "pair"), part)

    for way in (1, -1):
        @pl.when(inner)
        def _(way=way):
            first = 0 if way == 1 else ROWS
            wires.arrive(("cols", way), ucols.at[pl.ds(first, ROWS)])

    def source(child, parent_tile):
        row = y * 2 + child
        where, found = jnp.int32(0), jnp.int32(0)
        for position in range(8):
            hit = (ext_ref[row, position] == parent_tile).astype(jnp.int32)
            where, found = jnp.where(hit > 0, position, where), found + hit
        return where, found.astype(F32)

    g_high[...], g_low[...] = split(gbuf[...])
    columns = []
    for child in range(2):
        where, found = source(child, 2 + column_tile)
        columns.append(cbuf[child, where, pl.ds(col_rows, 128), :] * found)
        for pivot in range(2):
            where, found = source(child, jnp.int32(pivot))
            p_high[pivot, child], p_low[pivot, child] = split(cbuf[child, where] * found)
    hat = []
    for pivot in range(2):
        part = ucols[:, pivot * 256 : (pivot + 1) * 256]
        for child in range(2):
            part = part - dot3(nt, columns[child], p_high[pivot, child], p_low[pivot, child])
        hat.append(part)
    weight = dot3(nt, jnp.concatenate(hat, axis=1), g_high[...], g_low[...])
    back = dot3(nn, weight, g_high[...], g_low[...])
    y_cat[...] = stack(back)
    for child in range(2):
        total = columns[child]
        for pivot in range(2):
            total = total - dot3(
                nn, back[:, pivot * 256 : (pivot + 1) * 256], p_high[pivot, child], p_low[pivot, child]
            )
        b_cat[child] = stack(total)

    loads[4].wait()

    def times(value, right):
        value_high, value_low = split(value)
        wide = nt(value_high, right)
        return wide[:, :128] + wide[:, 128:] + nt(value_low, right[:128])

    for index in range(8):
        total = block_v[pl.ds(index * TILE, TILE), :] - times(ubuf[index], y_cat[...])
        for child in range(2):
            where, found = source(child, 2 + low * 8 + index)
            total = total - times(cbuf[child, where], b_cat[child]) * found
        out_v[pl.ds(index * TILE, TILE), :] = total
        pltpu.make_async_copy(
            out_v.at[pl.ds(index * TILE, TILE)], out_ref.at[0, pl.ds(index * TILE, TILE)], out_sems.at[index]
        ).start()

    wires.drain()
    for way in (1, -1):
        @pl.when(cols_needed((x + way + NX) % NX))
        def _(way=way):
            cols_copy(way).wait_send()
    for index in range(8):
        pltpu.make_async_copy(
            out_v.at[pl.ds(index * TILE, TILE)], out_ref.at[0, pl.ds(index * TILE, TILE)], out_sems.at[index]
        ).wait()


def local(panel, pattern, child_inverse, ext_map, upper_rows, parent_inverse, update_block):
    smem = pl.BlockSpec(memory_space=pltpu.SMEM)
    anywhere = pl.BlockSpec(memory_space=pl.ANY)
    return pl.pallas_call(
        kernel,
        out_shape=jax.ShapeDtypeStruct((1, 2048, 128), F32),
        in_specs=[smem, smem] + [anywhere] * 5,
        out_specs=anywhere,
        scratch_shapes=[
            pltpu.VMEM((2, 8, TILE, 512), F32),
            pltpu.VMEM((8, TILE, 512), F32),
            pltpu.VMEM((128, 512), F32),
            pltpu.VMEM((512, 512), F32),
            pltpu.VMEM((ROWS, 512), F32),
            pltpu.VMEM((512, 512), F32),
            pltpu.VMEM((2048, 128), F32),
            pltpu.VMEM((2048, 128), F32),
            pltpu.VMEM((2, 2, TILE, 512), BF16),
            pltpu.VMEM((2, 2, TILE, 512), BF16),
            pltpu.VMEM((512, 512), BF16),
            pltpu.VMEM((512, 512), BF16),
            pltpu.VMEM((2, 256, 512), BF16),
            pltpu.VMEM((256, 512), BF16),
            pltpu.SemaphoreType.DMA((5,)),
            pltpu.SemaphoreType.DMA((8,)),
            pltpu.SemaphoreType.DMA((160,)),
            pltpu.SemaphoreType.DMA((160,)),
        ],
        compiler_params=pltpu.CompilerParams(
            collective_id=0, has_side_effects=True, vmem_limit_bytes=52 * 2**20
        ),
    )(ext_map, pattern, panel, child_inverse, upper_rows, parent_inverse, update_block)


def solution(mesh):
    in_specs = (
        P("cube", "grid", None),
        P("cube", None, None),
        P("cube", None, None),
        P(),
        P("cube", "grid", None),
        P("cube", None, None),
        P("cube", None, "grid"),
    )
    out_specs = P("cube", None, "grid")
    return jax.shard_map(local, mesh=mesh, in_specs=in_specs, out_specs=out_specs, check_vma=False)
```

time: 426 us -> 69.4 us (0.16)
  the two profiles are of different devices: /device:TPU:1 before, /device:TPU:18 now
where the time goes in v1:
time: 69.4 us; the launch traced here: 69.2 us
  Pallas kernels  64.5 us (93%)
  local copies, waits for them, and re-layouts  4.59 us (7%)
    pallas_call x1, Pallas kernels, local(): pl.pallas_call(kernel, out_shape=jax.ShapeDtypeStruct((1, 2048, 128), F32...  64.5 us
    unnamed x10, local copies, waits for them, and re-layouts  4.59 us

profile of v1, /device:TPU:18, one launch (start us, length us, event | category | flops | bytes accessed | tf_op | source)
XLA Modules:
  0.0 69.2 jit_solution(13529102688779381853)
XLA Ops:
  0.0 0.0 copy-start.3
  0.0 0.8 %copy.8.pat_ref = s32[1,8,2]{2,1,0:T(8,128)S(1)} copy(s32[1,8,2]{1,2,0:T(2,128)} %param.8) | data formatting | bytes 128 | tf_op args[1]
  0.8 0.0 copy-done.3
  0.8 0.0 copy-start
  0.8 1.0 %copy-done = f32[1,256,512]{2,1,0:T(8,128)S(1)} copy-done((f32[1,256,512]{2,1,0:T(8,128)S(1)}, f32[1,256,512]{2,1,0:T(8,128)}, u32[]{:S(2)}) %copy-start) | copy-done | bytes 524312
  1.8 0.0 copy-start.1
  1.8 0.9 %copy-done.1 = f32[1,64,512]{2,1,0:T(8,128)S(1)} copy-done((f32[1,64,512]{2,1,0:T(8,128)S(1)}, f32[1,64,512]{2,1,0:T(8,128)}, u32[]{:S(2)}) %copy-start.1) | copy-done | bytes 131096
  2.7 0.0 copy-start.2
  2.7 0.9 %copy-done.2 = f32[1,64,512]{2,1,0:T(8,128)S(1)} copy-done((f32[1,64,512]{2,1,0:T(8,128)S(1)}, f32[1,64,512]{2,1,0:T(8,128)}, u32[]{:S(2)}) %copy-start.2) | copy-done | bytes 131096
  3.6 64.5 %shard_map.73 = f32[1,2048,128]{2,1,0:T(8,128)S(1)} custom-call(s32[8,8]{1,0:T(8,128)S(1)} %copy-done.3, s32[1,8,2]{2,1,0:T(8,128)S(1)} %copy.8.pat_ref, f32[1,64,512]{2,1,0:T(8,128)S(1)} %copy-done.1, f32[1,512,512]{2,1,0:T(8,128)} %cinv_ref.1, f32[1,64,512]{2,1,0:T(8,128)S(1)} %copy-done.2, f32[1,256,512]{2,1,0:T(8,128)S(1)} %copy-done, ...), custom_call_target="tpu_custom_call" | custom-call | tf_op jit(solution)/shard_map/pallas_call | solution.py:347
  68.2 1.0 %copy.10 = f32[1,2048,128]{2,1,0:T(8,128)} copy(f32[1,2048,128]{2,1,0:T(8,128)S(1)} %shard_map.73) | data formatting | bytes 2097152
Async XLA Ops:
  0.0 0.8 %copy-start.3 = (s32[8,8]{1,0:T(8,128)S(1)}, s32[8,8]{1,0:T(8,128)}, u32[]{:S(2)}) copy-start(s32[8,8]{1,0:T(8,128)} %ext_ref.1) | copy-start | bytes 772
  0.8 1.0 %copy-start = (f32[1,256,512]{2,1,0:T(8,128)S(1)}, f32[1,256,512]{2,1,0:T(8,128)}, u32[]{:S(2)}) copy-start(f32[1,256,512]{2,1,0:T(8,128)} %pinv_ref.1) | copy-start | bytes 1572868
  1.8 0.9 %copy-start.1 = (f32[1,64,512]{2,1,0:T(8,128)S(1)}, f32[1,64,512]{2,1,0:T(8,128)}, u32[]{:S(2)}) copy-start(f32[1,64,512]{2,1,0:T(8,128)} %panel_ref.1) | copy-start | bytes 393220
  2.7 0.9 %copy-start.2 = (f32[1,64,512]{2,1,0:T(8,128)S(1)}, f32[1,64,512]{2,1,0:T(8,128)}, u32[]{:S(2)}) copy-start(f32[1,64,512]{2,1,0:T(8,128)} %upper_ref.1) | copy-start | bytes 393220

commit v2 on v1

v2 whole, which is shorter than its diff:
```python
import jax
import jax.numpy as jnp
from jax import lax
from jax.experimental import pallas as pl
from jax.experimental.pallas import tpu as pltpu
from jax.sharding import PartitionSpec as P

MESH = pl.DeviceIdType.MESH
F32 = jnp.float32
BF16 = jnp.bfloat16
NX, NZ = 4, 8
ROWS = 64
CUT = 48
WEIGHT = {"a": 0.0, "b": -4.0, "u": 0.0, "g": 0.0, "cols": 0.0}
TILE = 256


def nt(left, right):
    return lax.dot_general(left, right, (((1,), (1,)), ((), ())), preferred_element_type=F32)


def nn(left, right):
    return lax.dot_general(left, right, (((1,), (0,)), ((), ())), preferred_element_type=F32)


def split(value):
    high = value.astype(BF16)
    return high, (value - high.astype(F32)).astype(BF16)


def stack(value):
    return jnp.concatenate(split(value), axis=0)


def dot3(mul, left, right_high, right_low):
    count = left.shape[0]
    both = stack(left)
    wide = mul(both, right_high)
    return wide[:count] + wide[count:] + mul(both[:count], right_low)


WAYS = (1, -1)
LAST = NZ // 2
TAIL = ROWS - CUT
ROW_TIME, LATENCY, AHEAD, STEP = 0.0415, 2.0, 2.5, 0.05


def span(first, count, step, way):
    if step < LAST:
        return first, count
    return (first, count // 2) if way == 1 else (first + count // 2, count // 2)


def part(first, count, side, way):
    front = (count // 2 + (4 if way == 1 else 0)) // 8 * 8
    return (first, front) if side == 1 else (first + front, count - front)


def messages():
    table, after = {}, {}

    def add(name, links, count, *needs):
        table[name], after[name] = (links, count), needs

    def ring(base, needs, first, count):
        for way in WAYS:
            before = needs
            for step in range(1, LAST + 1):
                add(base + (way, step), (("z", way),), span(first, count, step, way)[1], *before)
                before = (base + (way, step),)

    ring(("a", "z"), ("C",), 0, CUT)
    for step in range(LAST + 1):
        for way in WAYS if step else (1,):
            first, count = span(0, CUT, step, way)
            for side in WAYS:
                near = ("a", step, way, "x", side)
                add(near, (("x", side),), count, ("a", "z", way, step) if step else "C")
                add(near[:3] + ("xx", side), (("x", side),), part(first, count, side, way)[1], near)
    ring(("b", 0), ("C",), CUT, TAIL)
    for side in WAYS:
        add(("b", "x", side), (("x", side),), TAIL, "C")
        add(("b", "xx", side), (("x", side),), part(CUT, TAIL, side, 1)[1], ("b", "x", side))
        ring(("b", -side), (("b", "x", side),), CUT, TAIL)
    ring(("b", 2), (("b", "xx", 1), ("b", "xx", -1)), CUT, TAIL)
    ring(("u", 0), ("U",), 0, ROWS)
    add(("u", "far"), (("x", 1), ("x", -1)), ROWS, "U")
    ring(("u", 2), (("u", "far"),), 0, ROWS)
    rows_of_u = tuple(name for name in table if name[0] == "u")
    for side in WAYS:
        add(("g", side), (("x", side),), ROWS, "G")
        add(("cols", side), (("x", side),), ROWS, *rows_of_u)
    return table, after


def plan():
    table, after = messages()
    users = {}
    for name, needs in after.items():
        for need in needs:
            users.setdefault(need, []).append(name)
    chain = {}

    def length(name):
        if name not in chain:
            chain[name] = max(
                (length(user) + LATENCY + table[user][1] * ROW_TIME for user in users.get(name, ())), default=0.0
            )
        return chain[name]

    def rank(name):
        return length(name) + WEIGHT[name[0]]

    links = [(axis, way) for axis in "xz" for way in WAYS]
    free = {link: 0.0 for link in links}
    ready = []
    missing = {name: len(needs) for name, needs in after.items()}
    now, events, order = 0.0, [(0.0, 0, "U"), (0.0, 1, "C"), (0.0, 2, "G")], []
    number = 3
    while events:
        events.sort()
        time, _, name = events.pop(0)
        now = max(now, time) + 2 * STEP
        order.append(("wait", name))
        for user in users.get(name, ()):
            missing[user] -= 1
            if not missing[user]:
                ready.append(user)
        ready.sort(key=lambda user: -rank(user))
        for user in list(ready):
            over, count = table[user]
            if max(free[link] for link in over) - now > AHEAD:
                continue
            ready.remove(user)
            end = max([now] + [free[link] for link in over]) + count * ROW_TIME
            for link in over:
                free[link] = end
            events.append((end + LATENCY, number, user))
            number += 1
            order.append(("send", user))
            now += STEP
    assert not ready
    return order


class Wires:
    def __init__(self, send_sems, recv_sems, pair_sems, model, any_device):
        self.send_sems, self.recv_sems, self.pair_sems = send_sems, recv_sems, pair_sems
        self.model, self.any_device = model, any_device
        self.number, self.sent, self.paired = {}, {}, {}

    def copy(self, source, target, send_sem, recv_sem, device):
        return pltpu.make_async_remote_copy(
            src_ref=source,
            dst_ref=target,
            send_sem=send_sem,
            recv_sem=recv_sem,
            device_id=device,
            device_id_type=MESH,
        )

    def named(self, name):
        return self.recv_sems.at[self.number.setdefault(name, len(self.number))]

    def send(self, name, piece, device):
        self.copy(piece, piece, self.send_sems.at[0], self.named(name), device).start()
        self.sent[0] = self.sent.get(0, 0) + piece.shape[0]

    def arrive(self, name, piece):
        self.copy(piece, piece, self.send_sems.at[0], self.named(name), self.any_device).wait_recv()

    def pair(self, kind, piece):
        self.copy(piece, piece, self.send_sems.at[1], self.pair_sems.at[kind], self.any_device).start()
        self.sent[1] = self.sent.get(1, 0) + piece.shape[0]
        self.paired[kind] = self.paired.get(kind, 0) + piece.shape[0]

    def rows(self, count):
        for outer in (1, 2):
            for tiles in range(1, 9):
                if count % (outer * tiles * 8) == 0 and count // (outer * tiles) <= TILE:
                    return self.model.at[pl.ds(0, outer), pl.ds(0, tiles), pl.ds(0, count // (outer * tiles))]
        raise ValueError(count)

    def pair_arrive(self, kind):
        piece = self.rows(self.paired[kind])
        self.copy(piece, piece, self.send_sems.at[1], self.pair_sems.at[kind], self.any_device).wait_recv()

    def drain(self):
        for kind, count in self.sent.items():
            piece = self.rows(count)
            self.copy(piece, piece, self.send_sems.at[kind], self.pair_sems.at[0], self.any_device).wait_send()


def kernel(
    ext_hbm, pat_hbm, panel_ref, cinv_ref, upper_ref, pinv_ref, block_ref, out_ref,
    cbuf, ubuf, ucols, gbuf, panel_v, cinv_v, block_v,
    p_high, p_low, g_high, g_low, b_cat, y_cat, ext_ref, pat_ref,
    local_sems, send_sems, recv_sems, pair_sems, cols_sems,
):
    cube, grid = lax.axis_index("cube"), lax.axis_index("grid")
    y, low = cube // 2, cube % 2
    high, z, core = grid // 16, (grid % 16) // 2, grid % 2
    x = high * 2 + low

    def device(xx, zz, cc):
        return (y * 2 + xx % 2, (xx // 2) * 16 + zz * 2 + cc)

    sibling = device(x, z, 1 - core)
    x_next = {1: device((x + 1) % NX, z, core), -1: device((x + 3) % NX, z, core)}
    x_far = device((x + 2) % NX, z, core)
    z_next = {1: device(x, (z + 1) % NZ, core), -1: device(x, (z + 7) % NZ, core)}

    def rows_of(xx, zz, cc, first, count):
        tile = (xx // 2) * 4 + zz // 2
        start = pl.multiple_of((zz % 2) * 128 + cc * ROWS + first, 8)
        return tile, pl.ds(start, count)

    def c_slot(dx, dz, cc, first=0, count=ROWS):
        xx, zz = (x + dx + NX) % NX, (z + dz + NZ) % NZ
        tile, rows = rows_of(xx, zz, cc, first, count)
        return cbuf.at[xx % 2, tile, rows]

    def u_slot(dx, dz, cc, first=0, count=ROWS):
        xx, zz = (x + dx + NX) % NX, (z + dz + NZ) % NZ
        tile, rows = rows_of(xx, zz, cc, first, count)
        return ubuf.at[tile, rows]

    loads = [
        pltpu.make_async_copy(panel_ref.at[0], panel_v, local_sems.at[0]),
        pltpu.make_async_copy(cinv_ref.at[0], cinv_v, local_sems.at[1]),
        pltpu.make_async_copy(upper_ref.at[0], u_slot(0, 0, core), local_sems.at[2]),
        pltpu.make_async_copy(
            pinv_ref.at[0], gbuf.at[pl.ds(pl.multiple_of(low * 256, 256), 256)], local_sems.at[3]
        ),
        pltpu.make_async_copy(block_ref.at[0], block_v, local_sems.at[4]),
        pltpu.make_async_copy(pat_hbm, pat_ref, local_sems.at[5]),
        pltpu.make_async_copy(ext_hbm, ext_ref, local_sems.at[6]),
    ]
    for load in loads:
        load.start()

    barrier = pltpu.get_barrier_semaphore()
    greeted = [sibling, x_next[1], x_next[-1], x_far, z_next[1], z_next[-1]]
    for other in greeted:
        pl.semaphore_signal(barrier, inc=1, device_id=other, device_id_type=MESH)

    wires = Wires(send_sems, recv_sems, pair_sems, cbuf, sibling)
    def c_at(dx):
        return lambda dz, first, count: c_slot(dx, dz, core, first, count)

    def u_at(dx):
        return lambda dz, first, count: u_slot(dx, dz, core, first, count)

    def g_rows(half, way):
        start = half * 256 + (0 if way == 1 else 128) + core * 64
        return gbuf.at[pl.ds(pl.multiple_of(start, 64), 64)]

    def arrived(name):
        kind = name[0]
        if kind == "g":
            return g_rows(1 - low, name[1])
        if kind == "u":
            if name[1] == "far":
                return u_slot(2, 0, core)
            _, dx, way, step = name
            return u_slot(dx, -way * step, core, *span(0, ROWS, step, way))
        if kind == "a" and name[1] == "z":
            _, _, way, step = name
            return c_slot(0, -way * step, core, *span(0, CUT, step, way))
        if kind == "a":
            _, step, way, reach, side = name
            rows = span(0, CUT, step, way)
            if reach == "x":
                return c_slot(-side, -way * step, core, *rows)
            return c_slot(2, -way * step, core, *part(*rows, side, way))
        if name[1] == "x":
            return c_slot(-name[2], 0, core, CUT, TAIL)
        if name[1] == "xx":
            return c_slot(2, 0, core, *part(CUT, TAIL, name[2], 1))
        _, dx, way, step = name
        return c_slot(dx, -way * step, core, *span(CUT, TAIL, step, way))

    def leaving(name):
        kind = name[0]
        if kind == "g":
            return g_rows(low, name[1]), x_next[name[1]]
        if kind == "u":
            if name[1] == "far":
                return u_slot(0, 0, core), x_far
            _, dx, way, step = name
            return u_slot(dx, -way * (step - 1), core, *span(0, ROWS, step, way)), z_next[way]
        if kind == "a" and name[1] == "z":
            _, _, way, step = name
            return c_slot(0, -way * (step - 1), core, *span(0, CUT, step, way)), z_next[way]
        if kind == "a":
            _, step, way, reach, side = name
            rows = span(0, CUT, step, way)
            if reach == "x":
                return c_slot(0, -way * step, core, *rows), x_next[side]
            return c_slot(-side, -way * step, core, *part(*rows, side, way)), x_next[side]
        if name[1] == "x":
            return c_slot(0, 0, core, CUT, TAIL), x_next[name[2]]
        if name[1] == "xx":
            return c_slot(-name[2], 0, core, *part(CUT, TAIL, name[2], 1)), x_next[name[2]]
        _, dx, way, step = name
        return c_slot(dx, -way * (step - 1), core, *span(CUT, TAIL, step, way)), z_next[way]

    column_tile = high * 8 + z
    own_cols = low == high
    inner = jnp.logical_not(own_cols)
    col_rows = pl.multiple_of(core * 128, 128)

    def cols_copy(way):
        first = 0 if way == 1 else ROWS
        return wires.copy(
            ubuf.at[z, pl.ds(pl.multiple_of(col_rows + first, 64), ROWS)],
            ucols.at[pl.ds(first, ROWS)],
            cols_sems.at[0, 0 if way == 1 else 1],
            cols_sems.at[1, 0 if way == 1 else 1],
            x_next[way],
        )

    def cols_when(way):
        beside = (x + way + NX) % NX
        return pl.when(jnp.logical_or(beside == 1, beside == 2))

    loads[0].wait()
    loads[1].wait()
    loads[5].wait()
    own_tile = grid // 4
    keep = [pat_ref[0, side, own_tile].astype(F32) for side in range(2)]
    masked = jnp.concatenate([panel_v[:, :256] * keep[0], panel_v[:, 256:] * keep[1]], axis=1)
    inv_high, inv_low = split(cinv_v[...])
    tile, rows = rows_of(x, z, core, 0, ROWS)
    cbuf[low, tile, rows, :] = dot3(nt, masked, inv_high, inv_low)
    loads[2].wait()
    loads[3].wait()

    pl.semaphore_wait(barrier, len(greeted))

    pair_kind = {"a": 0, "b": 0, "u": 1, "g": 2}
    for action, name in plan():
        if action == "wait":
            if name == "U":
                wires.pair(1, u_slot(0, 0, core))
            elif name == "C":
                wires.pair(0, c_slot(0, 0, core))
            elif name[0] in pair_kind:
                piece = arrived(name)
                wires.arrive(name, piece)
                wires.pair(pair_kind[name[0]], piece)
        elif name[0] == "cols":
            if name[1] == 1:
                wires.pair_arrive(1)

                @pl.when(own_cols)
                def _():
                    ucols[...] = ubuf[z, pl.ds(col_rows, 128), :]

            @cols_when(name[1])
            def _(way=name[1]):
                cols_copy(way).start()
        else:
            wires.send(name, *leaving(name))

    wires.pair_arrive(2)
    wires.pair_arrive(0)
    for way in WAYS:
        @pl.when(inner)
        def _(way=way):
            cols_copy(way).wait_recv()

    loads[6].wait()

    def source(child, parent_tile):
        row = y * 2 + child
        where, found = jnp.int32(0), jnp.int32(0)
        for position in range(8):
            hit = (ext_ref[row, position] == parent_tile).astype(jnp.int32)
            where, found = jnp.where(hit > 0, position, where), found + hit
        return where, found.astype(F32)

    g_high[...], g_low[...] = split(gbuf[...])
    columns = []
    for child in range(2):
        where, found = source(child, 2 + column_tile)
        columns.append(cbuf[child, where, pl.ds(col_rows, 128), :] * found)
        for pivot in range(2):
            where, found = source(child, jnp.int32(pivot))
            p_high[pivot, child], p_low[pivot, child] = split(cbuf[child, where] * found)
    hat = []
    for pivot in range(2):
        minus = ucols[:, pivot * 256 : (pivot + 1) * 256]
        for child in range(2):
            minus = minus - dot3(nt, columns[child], p_high[pivot, child], p_low[pivot, child])
        hat.append(minus)
    weight = dot3(nt, jnp.concatenate(hat, axis=1), g_high[...], g_low[...])
    back = dot3(nn, weight, g_high[...], g_low[...])
    y_cat[...] = stack(back)
    for child in range(2):
        total = columns[child]
        for pivot in range(2):
            total = total - dot3(
                nn, back[:, pivot * 256 : (pivot + 1) * 256], p_high[pivot, child], p_low[pivot, child]
            )
        b_cat[child] = stack(total)

    loads[4].wait()

    def times(value, right):
        value_high, value_low = split(value)
        wide = nt(value_high, right)
        return wide[:, :128] + wide[:, 128:] + nt(value_low, right[:128])

    for index in range(8):
        total = block_v[pl.ds(index * TILE, TILE), :] - times(ubuf[index], y_cat[...])
        for child in range(2):
            where, found = source(child, 2 + low * 8 + index)
            total = total - times(cbuf[child, where], b_cat[child]) * found
        out_ref[0, pl.ds(index * TILE, TILE), :] = total

    wires.drain()
    for way in WAYS:
        @cols_when(way)
        def _(way=way):
            cols_copy(way).wait_send()


def local(panel, pattern, child_inverse, ext_map, upper_rows, parent_inverse, update_block):
    anywhere = pl.BlockSpec(memory_space=pltpu.HBM)
    return pl.pallas_call(
        kernel,
        out_shape=pltpu.VMEM((1, 2048, 128), F32),
        in_specs=[anywhere] * 7,
        out_specs=pl.BlockSpec(memory_space=pltpu.VMEM),
        scratch_shapes=[
            pltpu.VMEM((2, 8, TILE, 512), F32),
            pltpu.VMEM((8, TILE, 512), F32),
            pltpu.VMEM((128, 512), F32),
            pltpu.VMEM((512, 512), F32),
            pltpu.VMEM((ROWS, 512), F32),
            pltpu.VMEM((512, 512), F32),
            pltpu.VMEM((2048, 128), F32),
            pltpu.VMEM((2, 2, TILE, 512), BF16),
            pltpu.VMEM((2, 2, TILE, 512), BF16),
            pltpu.VMEM((512, 512), BF16),
            pltpu.VMEM((512, 512), BF16),
            pltpu.VMEM((2, 256, 512), BF16),
            pltpu.VMEM((256, 512), BF16),
            pltpu.SMEM((8, 8), jnp.int32),
            pltpu.SMEM((1, 2, 8), jnp.int32),
            pltpu.SemaphoreType.DMA((7,)),
            pltpu.SemaphoreType.DMA((2,)),
            pltpu.SemaphoreType.DMA((103,)),
            pltpu.SemaphoreType.DMA((3,)),
            pltpu.SemaphoreType.DMA((2, 2)),
        ],
        compiler_params=pltpu.CompilerParams(
            collective_id=0, has_side_effects=True, vmem_limit_bytes=60 * 2**20
        ),
    )(ext_map, jnp.swapaxes(pattern, 1, 2), panel, child_inverse, upper_rows, parent_inverse, update_block)


def solution(mesh):
    in_specs = (
        P("cube", "grid", None),
        P("cube", None, None),
        P("cube", None, None),
        P(),
        P("cube", "grid", None),
        P("cube", None, None),
        P("cube", None, "grid"),
    )
    out_specs = P("cube", None, "grid")
    return jax.shard_map(local, mesh=mesh, in_specs=in_specs, out_specs=out_specs, check_vma=False)
```

time: 69.4 us -> 59.5 us (0.86)
  the two profiles are of different devices: /device:TPU:18 before, /device:TPU:1 now
where the time goes in v2:
time: 59.5 us; the launch traced here: 59.4 us
  Pallas kernels  58.4 us (98%)
  local copies, waits for them, and re-layouts  0.97 us (2%)
    pallas_call x1, Pallas kernels, local(): pl.pallas_call(kernel, out_shape=pltpu.VMEM((1, 2048, 128), F32), in_spec...  58.4 us

profile of v2, /device:TPU:1, one launch (start us, length us, event | category | flops | bytes accessed | tf_op | source)
XLA Modules:
  0.0 59.4 jit_solution(741313368966731149)
XLA Ops:
  0.0 58.4 %shard_map.73 = f32[1,2048,128]{2,1,0:T(8,128)S(1)} custom-call(s32[8,8]{1,0:T(8,128)} %ext_hbm.1, s32[1,2,8]{2,1,0:T(2,128)} %bitcast.1, f32[1,64,512]{2,1,0:T(8,128)} %panel_ref.1, f32[1,512,512]{2,1,0:T(8,128)} %cinv_ref.1, f32[1,64,512]{2,1,0:T(8,128)} %upper_ref.1, f32[1,256,512]{2,1,0:T(8,128)} %pinv_ref.1, f32[1,2048,128]{2,1,0:T(8,128)} %block_ref.1), custom_call_target="tpu_custom_call" | custom-call | tf_op jit(solution)/shard_map/pallas_call | solution.py:431
  58.5 1.0 %copy.9 = f32[1,2048,128]{2,1,0:T(8,128)} copy(f32[1,2048,128]{2,1,0:T(8,128)S(1)} %shard_map.73) | data formatting | bytes 2097152

commit v3 on v2

v3 whole, which is shorter than its diff:
```python
import math

import jax
import jax.numpy as jnp
from jax import lax
from jax.experimental import pallas as pl
from jax.experimental.pallas import tpu as pltpu
from jax.sharding import PartitionSpec as P

MESH = pl.DeviceIdType.MESH
F32 = jnp.float32
BF16 = jnp.bfloat16
NX, NZ = 4, 8
ROWS = 64
CUT = 48
TILE = 256


def nt(left, right):
    return lax.dot_general(left, right, (((1,), (1,)), ((), ())), preferred_element_type=F32)


def nn(left, right):
    return lax.dot_general(left, right, (((1,), (0,)), ((), ())), preferred_element_type=F32)


def split(value):
    high = value.astype(BF16)
    return high, (value - high.astype(F32)).astype(BF16)


def stack(value):
    return jnp.concatenate(split(value), axis=0)


def dot3(mul, left, right_high, right_low):
    count = left.shape[0]
    both = stack(left)
    wide = mul(both, right_high)
    return wide[:count] + wide[count:] + mul(both[:count], right_low)


WAYS = (1, -1)
LAST = NZ // 2
TAIL = ROWS - CUT
ROW_TIME, LATENCY, AHEAD, STEP, READY = 0.043, 2.3, 2.5, 0.08, 2.0
PAIR = 1.0
WEIGHT = {("b", "z"): -4.0}


def span(first, count, step, way):
    if step < LAST:
        return first, count
    return (first, count // 2) if way == 1 else (first + count // 2, count // 2)


def part(first, count, side):
    front = max(count // 24, 1) * 8
    return (first, front) if side == 1 else (first + front, count - front)


def messages():
    table, after = {}, {}

    def add(name, links, count, *needs):
        table[name], after[name] = (links, count), needs

    def ring(base, needs, first, count, times=1):
        for way in WAYS:
            before = needs
            for step in range(1, LAST + 1):
                add(base + (way, step), (("z", way),), span(first, count, step, way)[1] * times, *before)
                before = (base + (way, step),)

    ring(("a", "z"), ("C",), 0, CUT)
    for step in range(LAST + 1):
        for way in WAYS if step else (1,):
            first, count = span(0, CUT, step, way)
            for side in WAYS:
                near = ("a", step, way, "x", side)
                add(near, (("x", side),), count, ("a", "z", way, step) if step else "C")
                add(near[:3] + ("xx", side), (("x", side),), part(first, count, side)[1], near)
    for side in WAYS:
        add(("b", "x", side), (("x", side),), TAIL, "C")
        add(("b", "xx", side), (("x", side),), part(CUT, TAIL, side)[1], ("b", "x", side))
    joined = tuple(("b", reach, side) for reach in ("x", "xx") for side in WAYS)
    ring(("b", "z"), joined, CUT, TAIL, NX)
    ring(("u", 0), ("U",), 0, ROWS)
    add(("u", "far"), (("x", 1), ("x", -1)), ROWS, "U")
    ring(("u", 2), (("u", "far"),), 0, ROWS)
    near_u = tuple(name for name in table if name[:2] == ("u", 0))
    for side in WAYS:
        add(("g", side), (("x", side),), ROWS, "G")
    add(("cols", "near"), (("x", 1),), 2 * ROWS, *near_u)
    return table, after


def work(table):
    def of(*kinds):
        return [name for name in table if name[0] in kinds]

    tasks = [("inverse", of("g"), 0.3), ("pivots", of("a", "b"), 0.5), ("hat", of("cols", "u"), 0.6)]
    tasks += [("weight", (), 0.5), ("back", (), 0.5), ("narrow", (), 0.5)]
    return tasks + [(("tile", index), (), 0.45) for index in range(8)]


def plan():
    table, after = messages()
    tasks, landed = work(table), {}
    users = {}
    for name, needs in after.items():
        for need in needs:
            users.setdefault(need, []).append(name)
    chain = {}

    def length(name):
        if name not in chain:
            chain[name] = max(
                (length(user) + LATENCY + table[user][1] * ROW_TIME for user in users.get(name, ())), default=0.0
            )
        return chain[name]

    def rank(name):
        return length(name) + WEIGHT.get(name[:2], 0.0)

    links = [(axis, way) for axis in "xz" for way in WAYS]
    free = {link: 0.0 for link in links}
    ready = []
    missing = {name: len(needs) for name, needs in after.items()}
    now, events, order = 0.0, [(0.0, 0, "U"), (0.1, 1, "G"), (READY, 2, "C")], []
    number = 3
    while events or tasks:
        events.sort()
        if tasks and all(need in landed for need in tasks[0][1]):
            start = max([0.0] + [landed[need] + PAIR for need in tasks[0][1]])
            if not events or max(start, now) < events[0][0]:
                now = max(start, now) + tasks[0][2]
                order.append(("work", tasks.pop(0)[0]))
                continue
        time, _, name = events.pop(0)
        now = max(now, time) + 2 * STEP
        landed[name] = now
        order.append(("wait", name))
        for user in users.get(name, ()):
            missing[user] -= 1
            if not missing[user]:
                ready.append(user)
        ready.sort(key=lambda user: -rank(user))
        for user in list(ready):
            over, count = table[user]
            if max(free[link] for link in over) - now > AHEAD:
                continue
            ready.remove(user)
            end = max([now] + [free[link] for link in over]) + count * ROW_TIME
            for link in over:
                free[link] = end
            events.append((end + LATENCY, number, user))
            number += 1
            order.append(("send", user))
            now += STEP
    assert not ready
    return order


def rows_in(piece):
    return math.prod(piece.shape[:-1])


class Wires:
    def __init__(self, send_sems, recv_sems, pair_sems, model, any_device):
        self.send_sems, self.recv_sems, self.pair_sems = send_sems, recv_sems, pair_sems
        self.model, self.any_device = model, any_device
        self.number, self.sent, self.paired = {}, {}, {}

    def copy(self, source, target, send_sem, recv_sem, device):
        return pltpu.make_async_remote_copy(
            src_ref=source,
            dst_ref=target,
            send_sem=send_sem,
            recv_sem=recv_sem,
            device_id=device,
            device_id_type=MESH,
        )

    def named(self, name):
        return self.recv_sems.at[self.number.setdefault(name, len(self.number))]

    def send(self, name, piece, device):
        piece, target = piece if isinstance(piece, tuple) else (piece, piece)
        self.copy(piece, target, self.send_sems.at[0], self.named(name), device).start()
        self.sent[0] = self.sent.get(0, 0) + rows_in(piece)

    def arrive(self, name, piece):
        self.copy(piece, piece, self.send_sems.at[0], self.named(name), self.any_device).wait_recv()

    def pair(self, kind, piece):
        self.copy(piece, piece, self.send_sems.at[1], self.pair_sems.at[kind], self.any_device).start()
        self.sent[1] = self.sent.get(1, 0) + rows_in(piece)
        self.paired[kind] = self.paired.get(kind, 0) + rows_in(piece)

    def rows(self, count):
        for tiles in (16, 8, 4, 3, 2, 1):
            if count % (8 * tiles) == 0 and count // tiles <= TILE:
                both, half, line = 2 if tiles > 8 else 1, 2 if tiles > 4 else 1, min(tiles, 4)
                return self.model.at[pl.ds(0, both), pl.ds(0, half), pl.ds(0, line), pl.ds(0, count // tiles)]
        raise ValueError(count)

    def pair_arrive(self, kind):
        piece = self.rows(self.paired[kind])
        self.copy(piece, piece, self.send_sems.at[1], self.pair_sems.at[kind], self.any_device).wait_recv()

    def drain(self):
        for kind, count in self.sent.items():
            piece = self.rows(count)
            self.copy(piece, piece, self.send_sems.at[kind], self.pair_sems.at[0], self.any_device).wait_send()


def kernel(
    ext_hbm, pat_hbm, panel_ref, cinv_ref, upper_ref, pinv_ref, block_ref, out_ref,
    cbuf, ubuf, ucols, fcols, hats, weights, gbuf, panel_v, cinv_v, block_v,
    p_high, p_low, g_high, g_low, b_cat, y_cat, ext_ref, pat_ref,
    local_sems, send_sems, recv_sems, pair_sems, cols_sems,
):
    cube, grid = lax.axis_index("cube"), lax.axis_index("grid")
    y, low = cube // 2, cube % 2
    high, z, core = grid // 16, (grid % 16) // 2, grid % 2
    x = high * 2 + low

    def device(xx, zz, cc):
        return (y * 2 + xx % 2, (xx // 2) * 16 + zz * 2 + cc)

    turn = jnp.where(z < NZ // 2, 1, -1)
    place = jnp.where(z < NZ // 2, x, NX - 1 - x)

    def across(dx):
        return (x + dx * turn + NX) % NX

    sibling = device(x, z, 1 - core)
    x_next = {1: device(across(1), z, core), -1: device(across(-1), z, core)}
    x_cross = {1: device(across(1), z, 1 - core), -1: device(across(-1), z, 1 - core)}
    x_far = device((x + 2) % NX, z, core)
    z_next = {1: device(x, (z + 1) % NZ, core), -1: device(x, (z + 7) % NZ, core)}

    def rows_of(zz, cc, first, count):
        return pl.ds(pl.multiple_of((zz % 2) * 128 + cc * ROWS + first, 8), count)

    def c_slot(dx, dz, cc, first=0, count=ROWS):
        xx, zz = across(dx), (z + dz + NZ) % NZ
        return cbuf.at[xx % 2, xx // 2, zz // 2, rows_of(zz, cc, first, count)]

    def c_line(dz, cc, first, count):
        zz = (z + dz + NZ) % NZ
        return cbuf.at[:, :, zz // 2, rows_of(zz, cc, first, count)]

    def u_slot(far, dz, cc, first=0, count=ROWS):
        zz = (z + dz + NZ) % NZ
        return ubuf.at[1 if far else 0, zz // 2, rows_of(zz, cc, first, count)]

    loads = [
        pltpu.make_async_copy(panel_ref.at[0], panel_v, local_sems.at[0]),
        pltpu.make_async_copy(cinv_ref.at[0], cinv_v, local_sems.at[1]),
        pltpu.make_async_copy(upper_ref.at[0], u_slot(0, 0, core), local_sems.at[2]),
        pltpu.make_async_copy(
            pinv_ref.at[0], gbuf.at[pl.ds(pl.multiple_of(low * 256, 256), 256)], local_sems.at[3]
        ),
        pltpu.make_async_copy(block_ref.at[0], block_v, local_sems.at[4]),
        pltpu.make_async_copy(pat_hbm, pat_ref, local_sems.at[5]),
        pltpu.make_async_copy(ext_hbm, ext_ref, local_sems.at[6]),
    ]
    for load in loads:
        load.start()

    barrier = pltpu.get_barrier_semaphore()
    greeted = [sibling, x_next[1], x_next[-1], x_cross[1], x_cross[-1], x_far, z_next[1], z_next[-1]]
    for other in greeted:
        pl.semaphore_signal(barrier, inc=1, device_id=other, device_id_type=MESH)

    wires = Wires(send_sems, recv_sems, pair_sems, cbuf, sibling)
    def c_at(dx):
        return lambda dz, first, count: c_slot(dx, dz, core, first, count)

    def u_at(dx):
        return lambda dz, first, count: u_slot(dx, dz, core, first, count)

    def g_rows(half, way):
        start = half * 256 + (0 if way == 1 else 128) + core * 64
        return gbuf.at[pl.ds(pl.multiple_of(start, 64), 64)]

    def arrived(name):
        kind = name[0]
        if kind == "g":
            return g_rows(1 - low, name[1])
        if kind == "u":
            if name[1] == "far":
                return u_slot(2, 0, core)
            _, dx, way, step = name
            return u_slot(dx, -way * step, core, *span(0, ROWS, step, way))
        if kind == "a" and name[1] == "z":
            _, _, way, step = name
            return c_slot(0, -way * step, core, *span(0, CUT, step, way))
        if kind == "a":
            _, step, way, reach, side = name
            rows = span(0, CUT, step, way)
            if reach == "x":
                return c_slot(-side, -way * step, core, *rows)
            return c_slot(2, -way * step, core, *part(*rows, side))
        if name[1] == "x":
            return c_slot(-name[2], 0, core, CUT, TAIL)
        if name[1] == "xx":
            return c_slot(2, 0, core, *part(CUT, TAIL, name[2]))
        _, _, way, step = name
        return c_line(-way * step, core, *span(CUT, TAIL, step, way))

    def leaving(name):
        kind = name[0]
        if kind == "g":
            return g_rows(low, name[1]), x_next[name[1]]
        if kind == "u":
            if name[1] == "far":
                return (u_slot(0, 0, core), u_slot(2, 0, core)), x_far
            _, dx, way, step = name
            return u_slot(dx, -way * (step - 1), core, *span(0, ROWS, step, way)), z_next[way]
        if kind == "a" and name[1] == "z":
            _, _, way, step = name
            return c_slot(0, -way * (step - 1), core, *span(0, CUT, step, way)), z_next[way]
        if kind == "a":
            _, step, way, reach, side = name
            rows = span(0, CUT, step, way)
            if reach == "x":
                return c_slot(0, -way * step, core, *rows), x_next[side]
            return c_slot(-side, -way * step, core, *part(*rows, side)), x_next[side]
        if name[1] == "x":
            return c_slot(0, 0, core, CUT, TAIL), x_next[name[2]]
        if name[1] == "xx":
            return c_slot(-name[2], 0, core, *part(CUT, TAIL, name[2])), x_next[name[2]]
        _, _, way, step = name
        return c_line(-way * (step - 1), core, *span(CUT, TAIL, step, way)), z_next[way]

    col_rows = pl.multiple_of(core * 128, 128)

    def cols_near(to_core):
        return wires.copy(
            ubuf.at[0, z % 4, pl.ds(pl.multiple_of(to_core * 128 + core * ROWS, ROWS), ROWS)],
            ucols.at[pl.ds(pl.multiple_of(core * ROWS, ROWS), ROWS)],
            cols_sems.at[0, to_core],
            cols_sems.at[1, core],
            device(across(1), z, to_core),
        )

    def cols_arrive():
        for from_core in range(2):
            piece = ucols.at[pl.ds(from_core * ROWS, ROWS)]
            wires.copy(piece, piece, cols_sems.at[0, 0], cols_sems.at[1, from_core], sibling).wait_recv()

    def own_panel():
        loads[0].wait()
        loads[1].wait()
        loads[5].wait()
        own_tile = grid // 4
        keep = [pat_ref[0, side, own_tile].astype(F32) for side in range(2)]
        masked = jnp.concatenate([panel_v[:, :256] * keep[0], panel_v[:, 256:] * keep[1]], axis=1)
        inv_high, inv_low = split(cinv_v[...])
        cbuf[low, high, z // 2, rows_of(z, core, 0, ROWS), :] = dot3(nt, masked, inv_high, inv_low)

    pl.semaphore_wait(barrier, len(greeted))

    def source(child, parent_tile):
        row = y * 2 + child
        side, line, found = jnp.int32(0), jnp.int32(0), jnp.int32(0)
        for position in range(8):
            hit = ext_ref[row, position] == parent_tile
            side, line = jnp.where(hit, position // 4, side), jnp.where(hit, position % 4, line)
            found = jnp.where(hit, 1, found)
        return side, line, found.astype(F32)

    def inverse():
        wires.pair_arrive(2)
        g_high[...], g_low[...] = split(gbuf[...])

    def pivots():
        wires.pair_arrive(0)
        loads[6].wait()
        for child in range(2):
            side, line, found = source(child, 2 + high * 8 + z)
            fcols[child] = cbuf[child, side, line, pl.ds(col_rows, 128), :] * found
            for pivot in range(2):
                side, line, found = source(child, jnp.int32(pivot))
                p_high[pivot, child], p_low[pivot, child] = split(cbuf[child, side, line] * found)

    def hat():
        wires.pair_arrive(1)
        wires.pair_arrive(3)
        for where, far in ((0, 0), (3, 1)):
            @pl.when(place == where)
            def _(far=far):
                ucols[...] = ubuf[far, z % 4, pl.ds(col_rows, 128), :]

        for pivot in range(2):
            total = ucols[:, pivot * 256 : (pivot + 1) * 256]
            for child in range(2):
                total = total - dot3(nt, fcols[child], p_high[pivot, child], p_low[pivot, child])
            hats[:, pivot * 256 : (pivot + 1) * 256] = total

    def weight():
        weights[...] = dot3(nt, hats[...], g_high[...], g_low[...])

    def back():
        hats[...] = dot3(nn, weights[...], g_high[...], g_low[...])
        y_cat[...] = stack(hats[...])

    def narrow():
        for child in range(2):
            total = fcols[child]
            for pivot in range(2):
                total = total - dot3(
                    nn, hats[:, pivot * 256 : (pivot + 1) * 256], p_high[pivot, child], p_low[pivot, child]
                )
            b_cat[child] = stack(total)
        loads[4].wait()

    def times(value, right):
        value_high, value_low = split(value)
        wide = nt(value_high, right)
        return wide[:, :128] + wide[:, 128:] + nt(value_low, right[:128])

    def tile(index):
        at = (high * 4 + index) % 8
        rows = pl.ds(pl.multiple_of(at * TILE, TILE), TILE)
        total = block_v[rows, :] - times(ubuf[index // 4, index % 4], y_cat[...])
        for child in range(2):
            side, line, found = source(child, 2 + low * 8 + at)
            total = total - times(cbuf[child, side, line], b_cat[child]) * found
        out_ref[0, rows, :] = total

    computing = dict(
        inverse=inverse, pivots=pivots, hat=hat, weight=weight, back=back, narrow=narrow,
        tile=tile,
    )

    held, lines = [], {}

    def release():
        for item in held:
            wires.pair(*item)
        held.clear()

    def pair_kind(name):
        if name[0] == "u":
            return 1 if name[1] == 0 else 3
        return 2 if name[0] == "g" else 0

    for action, name in plan():
        if action == "work":
            release()
            if isinstance(name, tuple):
                computing[name[0]](name[1])
            else:
                computing[name]()
        elif action == "wait":
            release()
            if name == "U":
                loads[2].wait()
                held.append((1, u_slot(0, 0, core)))
            elif name == "G":
                loads[3].wait()
            elif name == "C":
                own_panel()
            elif name == ("cols", "near"):
                pl.when(jnp.logical_or(place == 1, place == 2))(cols_arrive)
            else:
                piece = arrived(name)
                wires.arrive(name, piece)
                if name[0] in "ab" and name[1] != "z":
                    line, rows = (name[1:3], (0, CUT)) if name[0] == "a" else ((0, 1), (CUT, TAIL))
                    lines[line, rows] = lines.get((line, rows), 0) + 1
                    if lines[line, rows] == 4:
                        step, way = line
                        held.append((0, c_line(-way * step, core, *span(*rows, step, way))))
                elif name[:2] != ("a", "z"):
                    held.append((pair_kind(name), piece))
        elif name == ("cols", "near"):
            @pl.when(place < 2)
            def _():
                for to_core in range(2):
                    cols_near(to_core).start()
        else:
            wires.send(name, *leaving(name))

    wires.drain()

    @pl.when(place < 2)
    def _():
        for to_core in range(2):
            cols_near(to_core).wait_send()


def local(panel, pattern, child_inverse, ext_map, upper_rows, parent_inverse, update_block):
    anywhere = pl.BlockSpec(memory_space=pltpu.HBM)
    return pl.pallas_call(
        kernel,
        out_shape=pltpu.VMEM((1, 2048, 128), F32),
        in_specs=[anywhere] * 7,
        out_specs=pl.BlockSpec(memory_space=pltpu.VMEM),
        scratch_shapes=[
            pltpu.VMEM((2, 2, 4, TILE, 512), F32),
            pltpu.VMEM((2, 4, TILE, 512), F32),
            pltpu.VMEM((128, 512), F32),
            pltpu.VMEM((2, 128, 512), F32),
            pltpu.VMEM((128, 512), F32),
            pltpu.VMEM((128, 512), F32),
            pltpu.VMEM((512, 512), F32),
            pltpu.VMEM((ROWS, 512), F32),
            pltpu.VMEM((512, 512), F32),
            pltpu.VMEM((2048, 128), F32),
            pltpu.VMEM((2, 2, TILE, 512), BF16),
            pltpu.VMEM((2, 2, TILE, 512), BF16),
            pltpu.VMEM((512, 512), BF16),
            pltpu.VMEM((512, 512), BF16),
            pltpu.VMEM((2, 256, 512), BF16),
            pltpu.VMEM((256, 512), BF16),
            pltpu.SMEM((8, 8), jnp.int32),
            pltpu.SMEM((1, 2, 8), jnp.int32),
            pltpu.SemaphoreType.DMA((7,)),
            pltpu.SemaphoreType.DMA((2,)),
            pltpu.SemaphoreType.DMA((len(messages()[0]) - 1,)),
            pltpu.SemaphoreType.DMA((4,)),
            pltpu.SemaphoreType.DMA((2, 2)),
        ],
        compiler_params=pltpu.CompilerParams(
            collective_id=0, has_side_effects=True, vmem_limit_bytes=60 * 2**20
        ),
    )(ext_map, jnp.swapaxes(pattern, 1, 2), panel, child_inverse, upper_rows, parent_inverse, update_block)


def solution(mesh):
    in_specs = (
        P("cube", "grid", None),
        P("cube", None, None),
        P("cube", None, None),
        P(),
        P("cube", "grid", None),
        P("cube", None, None),
        P("cube", None, "grid"),
    )
    out_specs = P("cube", None, "grid")
    return jax.shard_map(local, mesh=mesh, in_specs=in_specs, out_specs=out_specs, check_vma=False)
```

time: 59.5 us -> 58 us (0.975)
  Pallas kernels: 58.4 us -> 56.9 us
    pallas_call x1, Pallas kernels: 58.4 us -> 56.9 us  [local(): pl.pallas_call(kernel, out_shape=pltpu.VMEM((1, 2048, 128), F32), in_spec...]
where the time goes in v3:
time: 58 us; the launch traced here: 57.9 us
  Pallas kernels  56.9 us (98%)
  local copies, waits for them, and re-layouts  0.97 us (2%)
    pallas_call x1, Pallas kernels, local(): pl.pallas_call(kernel, out_shape=pltpu.VMEM((1, 2048, 128), F32), in_spec...  56.9 us

profile of v3, /device:TPU:1, one launch (start us, length us, event | category | flops | bytes accessed | tf_op | source)
XLA Modules:
  0.0 57.9 jit_solution(11433300005203925139)
XLA Ops:
  0.0 56.9 %shard_map.73 = f32[1,2048,128]{2,1,0:T(8,128)S(1)} custom-call(s32[8,8]{1,0:T(8,128)} %ext_hbm.1, s32[1,2,8]{2,1,0:T(2,128)} %bitcast.1, f32[1,64,512]{2,1,0:T(8,128)} %panel_ref.1, f32[1,512,512]{2,1,0:T(8,128)} %cinv_ref.1, f32[1,64,512]{2,1,0:T(8,128)} %upper_ref.1, f32[1,256,512]{2,1,0:T(8,128)} %pinv_ref.1, f32[1,2048,128]{2,1,0:T(8,128)} %block_ref.1), custom_call_target="tpu_custom_call" | custom-call | tf_op jit(solution)/shard_map/pallas_call | solution.py:499
  56.9 1.0 %copy.9 = f32[1,2048,128]{2,1,0:T(8,128)} copy(f32[1,2048,128]{2,1,0:T(8,128)S(1)} %shard_map.73) | data formatting | bytes 2097152

commit v4 on v3

--- a/solution.py
+++ b/solution.py
@@ -43,9 +43,9 @@
 WAYS = (1, -1)
 LAST = NZ // 2
 TAIL = ROWS - CUT
-ROW_TIME, LATENCY, AHEAD, STEP, READY = 0.043, 2.3, 2.5, 0.08, 2.0
+ROW_TIME, LATENCY, AHEAD, STEP, READY = 0.043, 2.3, 2.4, 0.08, 1.5
 PAIR = 1.0
-WEIGHT = {("b", "z"): -4.0}
+WEIGHT = {("b", "z"): -4.0, ("a", "z"): 3.0}
 
 
 def span(first, count, step, way):
@@ -470,7 +470,9 @@
             else:
                 piece = arrived(name)
                 wires.arrive(name, piece)
-                if name[0] in "ab" and name[1] != "z":
+                if name[0] == "a" and LAST in name[1:4]:
+                    held.append((0, piece))
+                elif name[0] in "ab" and name[1] != "z":
                     line, rows = (name[1:3], (0, CUT)) if name[0] == "a" else ((0, 1), (CUT, TAIL))
                     lines[line, rows] = lines.get((line, rows), 0) + 1
                     if lines[line, rows] == 4:

time: 58 us -> 57.7 us (level)
  no operation moved by 1% of the time
where the time goes in v4:
time: 57.7 us; the launch traced here: 57.6 us
  Pallas kernels  56.6 us (98%)
  local copies, waits for them, and re-layouts  0.97 us (2%)
    pallas_call x1, Pallas kernels, local(): pl.pallas_call(kernel, out_shape=pltpu.VMEM((1, 2048, 128), F32), in_spec...  56.6 us

profile of v4, /device:TPU:1, one launch (start us, length us, event | category | flops | bytes accessed | tf_op | source)
XLA Modules:
  0.0 57.6 jit_solution(5208562788233007720)
XLA Ops:
  0.0 56.6 %shard_map.73 = f32[1,2048,128]{2,1,0:T(8,128)S(1)} custom-call(s32[8,8]{1,0:T(8,128)} %ext_hbm.1, s32[1,2,8]{2,1,0:T(2,128)} %bitcast.1, f32[1,64,512]{2,1,0:T(8,128)} %panel_ref.1, f32[1,512,512]{2,1,0:T(8,128)} %cinv_ref.1, f32[1,64,512]{2,1,0:T(8,128)} %upper_ref.1, f32[1,256,512]{2,1,0:T(8,128)} %pinv_ref.1, f32[1,2048,128]{2,1,0:T(8,128)} %block_ref.1), custom_call_target="tpu_custom_call" | custom-call | tf_op jit(solution)/shard_map/pallas_call | solution.py:501
  56.7 1.0 %copy.9 = f32[1,2048,128]{2,1,0:T(8,128)} copy(f32[1,2048,128]{2,1,0:T(8,128)S(1)} %shard_map.73) | data formatting | bytes 2097152

commit v5 on v4

--- a/solution.py
+++ b/solution.py
@@ -183,6 +183,7 @@
         )
 
     def named(self, name):
+        name = name[:-1] if "xx" in name else name
         return self.recv_sems.at[self.number.setdefault(name, len(self.number))]
 
     def send(self, name, piece, device):
@@ -437,7 +438,7 @@
         tile=tile,
     )
 
-    held, lines = [], {}
+    held, lines, halves = [], {}, {}
 
     def release():
         for item in held:
@@ -469,13 +470,19 @@
                 pl.when(jnp.logical_or(place == 1, place == 2))(cols_arrive)
             else:
                 piece = arrived(name)
+                if "xx" in name:
+                    halves[name[:-1]] = halves.get(name[:-1], 0) + 1
+                    if halves[name[:-1]] == 1:
+                        continue
+                    step, way = name[1:3] if name[0] == "a" else (0, 1)
+                    piece = c_slot(2, -way * step, core, *span(*((0, CUT) if name[0] == "a" else (CUT, TAIL)), step, way))
                 wires.arrive(name, piece)
                 if name[0] == "a" and LAST in name[1:4]:
                     held.append((0, piece))
                 elif name[0] in "ab" and name[1] != "z":
                     line, rows = (name[1:3], (0, CUT)) if name[0] == "a" else ((0, 1), (CUT, TAIL))
                     lines[line, rows] = lines.get((line, rows), 0) + 1
-                    if lines[line, rows] == 4:
+                    if lines[line, rows] == 3:
                         step, way = line
                         held.append((0, c_line(-way * step, core, *span(*rows, step, way))))
                 elif name[:2] != ("a", "z"):
@@ -524,7 +531,7 @@
             pltpu.SMEM((1, 2, 8), jnp.int32),
             pltpu.SemaphoreType.DMA((7,)),
             pltpu.SemaphoreType.DMA((2,)),
-            pltpu.SemaphoreType.DMA((len(messages()[0]) - 1,)),
+            pltpu.SemaphoreType.DMA((len(messages()[0]) - 11,)),
             pltpu.SemaphoreType.DMA((4,)),
             pltpu.SemaphoreType.DMA((2, 2)),
         ],

time: 57.7 us -> 57.7 us (level)
  no operation moved by 1% of the time
where the time goes in v5:
time: 57.7 us; the launch traced here: 57.6 us
  Pallas kernels  56.6 us (98%)
  local copies, waits for them, and re-layouts  0.97 us (2%)
    pallas_call x1, Pallas kernels, local(): pl.pallas_call(kernel, out_shape=pltpu.VMEM((1, 2048, 128), F32), in_spec...  56.6 us

profile of v5, /device:TPU:1, one launch (start us, length us, event | category | flops | bytes accessed | tf_op | source)
XLA Modules:
  0.0 57.6 jit_solution(2798940579750275647)
XLA Ops:
  0.0 56.6 %shard_map.73 = f32[1,2048,128]{2,1,0:T(8,128)S(1)} custom-call(s32[8,8]{1,0:T(8,128)} %ext_hbm.1, s32[1,2,8]{2,1,0:T(2,128)} %bitcast.1, f32[1,64,512]{2,1,0:T(8,128)} %panel_ref.1, f32[1,512,512]{2,1,0:T(8,128)} %cinv_ref.1, f32[1,64,512]{2,1,0:T(8,128)} %upper_ref.1, f32[1,256,512]{2,1,0:T(8,128)} %pinv_ref.1, f32[1,2048,128]{2,1,0:T(8,128)} %block_ref.1), custom_call_target="tpu_custom_call" | custom-call | tf_op jit(solution)/shard_map/pallas_call | solution.py:508
  56.6 1.0 %copy.9 = f32[1,2048,128]{2,1,0:T(8,128)} copy(f32[1,2048,128]{2,1,0:T(8,128)S(1)} %shard_map.73) | data formatting | bytes 2097152
